TPU v7x, 512 devices: a whole 4x4x16 slice. The times are simulated.
512 devices in a mesh: cam: 16 (over z_lo, x), seq: 32 (over y, z_hi, core).
Axes of the slice: x: 4, y: 4, z: 16 (z_hi: 4, z_lo: 4; z = z_hi * 4 + z_lo), core: 2. Of those that a mesh axis runs over, the one named last changes fastest.
Arguments:
- queries: bfloat16 [16, 2048, 2048], P('cam', 'seq'), may hold values from -18 to 18
- keys: bfloat16 [16, 2048, 2048], P('cam', 'seq'), may hold values from -8 to 8
- values: bfloat16 [16, 2048, 2048], P('cam', 'seq'), may hold values from -6 to 6
- neighbour_mask: int32 [16, 4], replicated, may hold values from 0 to 1, as said below
Outputs:
- attended: bfloat16 [16, 2048, 2048], P('cam', 'seq')
Inputs may be any that keep to these rules, and one draw needn't show every extreme that they name: `neighbour_mask`: at least one camera has all 4 neighbours.
All inputs are finite; a program needn't handle non-finite values.
Results may differ from a plain program's by a relative error of at most 0.012.
Values may be sent and summed in bfloat16 or wider, within the bound.
No kernel may reach another device: no remote copies, remote signals or barrier semaphores. Data moves between devices by JAX's collectives and lax.ppermute only.
A program may use at most 64 MiB of HBM per device.

v0:
```python
import functools

import jax
import jax.numpy as jnp
from jax import lax
from jax.experimental import pallas as pl
from jax.experimental.pallas import tpu as pltpu
from jax.sharding import PartitionSpec as P

HEADS = 32
HD = 64
WIDE = 2 * HD
TILE = 256

VMEM = pl.BlockSpec(memory_space=pltpu.VMEM)
SMEM = pl.BlockSpec(memory_space=pltpu.SMEM)


def params(mib):
    return pltpu.CompilerParams(vmem_limit_bytes=mib << 20)


def pack_pairs_kernel(left_ref, right_ref, out_ref):
    for pair in range(HEADS // 2):
        left = left_ref[:, pair * WIDE : (pair + 1) * WIDE]
        right = right_ref[:, pair * WIDE : (pair + 1) * WIDE]
        out_ref[2 * pair] = jnp.concatenate([left[:, :HD], right[:, :HD]], axis=1)
        out_ref[2 * pair + 1] = jnp.concatenate([left[:, HD:], right[:, HD:]], axis=1)


def pack_keys_values(keys, values):
    rows = keys.shape[0]
    return pl.pallas_call(
        pack_pairs_kernel,
        out_shape=jax.ShapeDtypeStruct((HEADS, rows, WIDE), keys.dtype),
        in_specs=[VMEM, VMEM],
        out_specs=VMEM,
        compiler_params=params(16),
        name="pack_keys_values",
    )(keys, values)


def pack_queries_kernel(q_ref, out_ref):
    half = q_ref.shape[0] // 2
    pack_pairs_kernel(q_ref.at[pl.ds(0, half)], q_ref.at[pl.ds(half, half)], out_ref)


def pack_queries(queries):
    rows = queries.shape[0]
    return pl.pallas_call(
        pack_queries_kernel,
        out_shape=jax.ShapeDtypeStruct((HEADS, rows // 2, WIDE), queries.dtype),
        in_specs=[VMEM],
        out_specs=VMEM,
        compiler_params=params(16),
        name="pack_queries",
    )(queries)


def unpack_kernel(x_ref, out_ref):
    half = x_ref.shape[1]
    for pair in range(HEADS // 2):
        even, odd = x_ref[2 * pair], x_ref[2 * pair + 1]
        columns = pl.ds(pair * WIDE, WIDE)
        out_ref[pl.ds(0, half), columns] = jnp.concatenate([even[:, :HD], odd[:, :HD]], axis=1)
        out_ref[pl.ds(half, half), columns] = jnp.concatenate([even[:, HD:], odd[:, HD:]], axis=1)


def unpack_heads(x):
    return pl.pallas_call(
        unpack_kernel,
        out_shape=jax.ShapeDtypeStruct((2 * x.shape[1], HEADS * HD), x.dtype),
        in_specs=[VMEM],
        out_specs=VMEM,
        compiler_params=params(16),
        name="unpack_heads",
    )(x)


def tile_scores(q_ref, half, rows, keys):
    queries = q_ref[rows, half * HD : (half + 1) * HD] * jnp.bfloat16(HD**-0.5)
    return lax.dot_general(queries, keys, (((1,), (1,)), ((), ())), preferred_element_type=jnp.float32)


def halves(kv_ref):
    kv = kv_ref[...]
    lane = lax.broadcasted_iota(jnp.int32, kv.shape, 1)
    return kv[:, :HD], jnp.where(lane < HD, jnp.bfloat16(1), kv)


def tiles(q_ref):
    for start in range(0, q_ref.shape[0], TILE):
        for half in range(2):
            yield pl.ds(start, TILE), half


def first_kernel(q_ref, kv_ref, sums_ref, peaks_ref):
    keys, values = halves(kv_ref)
    for rows, half in tiles(q_ref):
        scores = tile_scores(q_ref, half, rows, keys)
        peak = jnp.max(scores, axis=1, keepdims=True)
        weights = jnp.exp(scores - peak).astype(jnp.bfloat16)
        sums_ref[half, rows] = jnp.dot(weights, values, preferred_element_type=jnp.float32)
        peaks_ref[half, rows] = jnp.broadcast_to(peak, (TILE, WIDE))


def next_kernel(column, enabled_ref, q_ref, kv_ref, old_sums_ref, old_peaks_ref, sums_ref, peaks_ref):
    @pl.when(enabled_ref[column] > 0)
    def _():
        keys, values = halves(kv_ref)
        for rows, half in tiles(q_ref):
            scores = tile_scores(q_ref, half, rows, keys)
            old_peak = old_peaks_ref[half, rows]
            peak = jnp.maximum(jnp.max(scores, axis=1, keepdims=True), old_peak)
            weights = jnp.exp(scores - peak[:, :1]).astype(jnp.bfloat16)
            added = jnp.dot(weights, values, preferred_element_type=jnp.float32)
            sums_ref[half, rows] = old_sums_ref[half, rows] * jnp.exp(old_peak - peak) + added
            peaks_ref[half, rows] = peak


def last_kernel(column, enabled_ref, q_ref, kv_ref, old_sums_ref, old_peaks_ref, out_ref):
    def store(rows, half, sums):
        out_ref[rows, half * HD : (half + 1) * HD] = (sums[:, HD:] / sums[:, :HD]).astype(out_ref.dtype)

    @pl.when(enabled_ref[column] > 0)
    def _():
        keys, values = halves(kv_ref)
        for rows, half in tiles(q_ref):
            scores = tile_scores(q_ref, half, rows, keys)
            old_peak = old_peaks_ref[half, rows]
            peak = jnp.maximum(jnp.max(scores, axis=1, keepdims=True), old_peak)
            weights = jnp.exp(scores - peak[:, :1]).astype(jnp.bfloat16)
            added = jnp.dot(weights, values, preferred_element_type=jnp.float32)
            store(rows, half, old_sums_ref[half, rows] * jnp.exp(old_peak - peak) + added)

    @pl.when(enabled_ref[column] <= 0)
    def _():
        for rows, half in tiles(q_ref):
            store(rows, half, old_sums_ref[half, rows])


def cost(q, kv):
    pairs = 2 * q.shape[0] * kv.shape[0]
    return pl.CostEstimate(flops=4 * pairs * HD, bytes_accessed=3 << 20, transcendentals=pairs)


def state_shape(q):
    return jax.ShapeDtypeStruct((2, q.shape[0], WIDE), jnp.float32)


def first_block(q, kv):
    return pl.pallas_call(
        first_kernel,
        out_shape=(state_shape(q), state_shape(q)),
        in_specs=[VMEM, VMEM],
        out_specs=(VMEM, VMEM),
        compiler_params=params(40),
        cost_estimate=cost(q, kv),
        name="own_camera",
    )(q, kv)


def next_block(column, enabled, q, kv, sums, peaks):
    return pl.pallas_call(
        functools.partial(next_kernel, column),
        out_shape=(state_shape(q), state_shape(q)),
        in_specs=[SMEM, VMEM, VMEM, VMEM, VMEM],
        out_specs=(VMEM, VMEM),
        input_output_aliases={3: 0, 4: 1},
        compiler_params=params(40),
        cost_estimate=cost(q, kv),
        name="next_camera",
    )(enabled, q, kv, sums, peaks)


def last_block(column, enabled, q, kv, sums, peaks):
    return pl.pallas_call(
        functools.partial(last_kernel, column),
        out_shape=jax.ShapeDtypeStruct(q.shape, q.dtype),
        in_specs=[SMEM, VMEM, VMEM, VMEM, VMEM],
        out_specs=VMEM,
        compiler_params=params(40),
        cost_estimate=cost(q, kv),
        name="last_camera",
    )(enabled, q, kv, sums, peaks)


def shifted(array, axis, by):
    devices = lax.axis_size(axis)
    return lax.ppermute(array, axis, [(i, (i + by) % devices) for i in range(devices)])


def on_device(queries, keys, values, neighbour_mask):
    own_row = lax.dynamic_index_in_dim(neighbour_mask, lax.axis_index("cam"), 0, keepdims=False)
    kv = pack_keys_values(keys[0], values[0])
    kv = lax.all_to_all(kv, "seq", split_axis=0, concat_axis=0, tiled=True).reshape(-1, WIDE)
    q = pack_queries(queries[0])
    shape = q.shape
    q = lax.all_to_all(q, "seq", split_axis=0, concat_axis=0, tiled=True).reshape(-1, WIDE)
    far = [shifted(kv, "cam", -1), shifted(kv, "cam", -2), shifted(kv, "cam", 1), shifted(kv, "cam", 2)]
    sums, peaks = first_block(q, kv)
    for column in (0, 2, 1):
        sums, peaks = next_block(column, own_row, q, far[column], sums, peaks)
    out = last_block(3, own_row, q, far[3], sums, peaks).reshape(shape)
    out = lax.all_to_all(out, "seq", split_axis=0, concat_axis=0, tiled=True)
    return unpack_heads(out)[None]


def solution(mesh):
    return jax.shard_map(
        on_device,
        mesh=mesh,
        in_specs=(P("cam", "seq", None), P("cam", "seq", None), P("cam", "seq", None), P()),
        out_specs=P("cam", "seq", None),
        check_vma=False,
    )
```

profile of v0, /device:TPU:33, one launch (start us, length us, event | category | flops | bytes accessed | tf_op | source)
XLA Modules:
  0.0 160.9 jit_solution(13650206752675488774)
XLA Ops:
  0.0 0.0 copy-start
  0.0 0.0 copy-start.2
  0.0 1.0 copy-done.2
  1.0 0.0 copy-start.3
  1.0 0.9 copy-done.3
  1.9 1.0 pack_keys_values.1
  2.9 0.0 copy-start.1
  2.9 17.8 %all-to-all-start.1 = ((bf16[32,64,128]{2,1,0:T(8,128)(2,1)}), bf16[32,64,128]{2,1,0:T(8,128)(2,1)S(1)}, u32[]{:S(2)}, u32[]{:S(2)}) async-start(bf16[32,64,128]{2,1,0:T(8,128)(2,1)} %pack_keys_values.1), calls=%async_computation.1 | async-start | bytes 1048576 | tf_op jit(solution)/shard_map/all_to_all | solution.py:196
  20.7 0.0 copy-done.1
  20.7 0.8 pack_queries.1
  21.6 34.0 %all-to-all-done.1 = bf16[32,64,128]{2,1,0:T(8,128)(2,1)S(1)} async-done(((bf16[32,64,128]{2,1,0:T(8,128)(2,1)}), bf16[32,64,128]{2,1,0:T(8,128)(2,1)S(1)}, u32[]{:S(2)}, u32[]{:S(2)}) %all-to-all-start.1) | async-done | bytes 524320 | tf_op jit(solution)/shard_map/all_to_all | solution.py:196
  55.6 3.8 %all-to-all-start = ((bf16[32,32,128]{2,1,0:T(8,128)(2,1)}), bf16[32,32,128]{2,1,0:T(8,128)(2,1)S(1)}, u32[]{:S(2)}, u32[]{:S(2)}) async-start(bf16[32,32,128]{2,1,0:T(8,128)(2,1)} %pack_queries.1), calls=%async_computation | async-start | bytes 524288 | tf_op jit(solution)/shard_map/all_to_all | solution.py:199
  59.4 3.1 %collective-permute-start.3 = (bf16[2048,128]{1,0:T(8,128)(2,1)S(1)}, bf16[2048,128]{1,0:T(8,128)(2,1)S(1)}, u32[]{:S(2)}, u32[]{:S(2)}) collective-permute-start(bf16[2048,128]{1,0:T(8,128)(2,1)S(1)} %bitcast.7), channel_id=1, source_target_pairs={{0,480},{32,0},{64,32},{96,64},{128,96},{160,128},{192,160},{224,1... | collective-permute-start | bytes 1572872 | tf_op jit(solution)/shard_map/ppermute | solution.py:190
  62.4 2.2 %collective-permute-start.2 = (bf16[2048,128]{1,0:T(8,128)(2,1)S(1)}, bf16[2048,128]{1,0:T(8,128)(2,1)S(1)}, u32[]{:S(2)}, u32[]{:S(2)}) collective-permute-start(bf16[2048,128]{1,0:T(8,128)(2,1)S(1)} %bitcast.8), channel_id=1, source_target_pairs={{0,32},{32,64},{64,96},{96,128},{128,160},{160,192},{192,224},{224... | collective-permute-start | bytes 1572872 | tf_op jit(solution)/shard_map/ppermute | solution.py:190
  64.7 3.3 %collective-permute-start.1 = (bf16[2048,128]{1,0:T(8,128)(2,1)S(1)}, bf16[2048,128]{1,0:T(8,128)(2,1)S(1)}, u32[]{:S(2)}, u32[]{:S(2)}) collective-permute-start(bf16[2048,128]{1,0:T(8,128)(2,1)S(1)} %bitcast.9), channel_id=1, source_target_pairs={{0,448},{32,480},{64,0},{96,32},{128,64},{160,96},{192,128},{224,1... | collective-permute-start | bytes 1572872 | tf_op jit(solution)/shard_map/ppermute | solution.py:190
  68.0 3.4 %collective-permute-start = (bf16[2048,128]{1,0:T(8,128)(2,1)S(1)}, bf16[2048,128]{1,0:T(8,128)(2,1)S(1)}, u32[]{:S(2)}, u32[]{:S(2)}) collective-permute-start(bf16[2048,128]{1,0:T(8,128)(2,1)S(1)} %bitcast.10), channel_id=1, source_target_pairs={{0,64},{32,96},{64,128},{96,160},{128,192},{160,224},{192,256},{22... | collective-permute-start | bytes 1572872 | tf_op jit(solution)/shard_map/ppermute | solution.py:190
  71.5 0.0 copy-done
  71.5 0.2 dynamic-slice_reduce_fusion.enabled_ref
  71.7 11.4 %all-to-all-done = bf16[32,32,128]{2,1,0:T(8,128)(2,1)S(1)} async-done(((bf16[32,32,128]{2,1,0:T(8,128)(2,1)}), bf16[32,32,128]{2,1,0:T(8,128)(2,1)S(1)}, u32[]{:S(2)}, u32[]{:S(2)}) %all-to-all-start) | async-done | bytes 262176 | tf_op jit(solution)/shard_map/all_to_all | solution.py:199
  83.0 5.9 %own_camera.1 = (f32[2,1024,128]{2,1,0:T(8,128)S(1)}, f32[2,1024,128]{2,1,0:T(8,128)S(1)}) custom-call(bf16[1024,128]{1,0:T(8,128)(2,1)S(1)} %bitcast.13, bf16[2048,128]{1,0:T(8,128)(2,1)S(1)} %bitcast.11), custom_call_target="tpu_custom_call" | custom-call | flops 1073741824 | bytes 3145728 | tf_op jit(solution)/shard_map/own_camera/pallas_call | solution.py:152
  89.0 3.1 %collective-permute-done.3.kv_ref = bf16[2048,128]{1,0:T(8,128)(2,1)S(1)} collective-permute-done((bf16[2048,128]{1,0:T(8,128)(2,1)S(1)}, bf16[2048,128]{1,0:T(8,128)(2,1)S(1)}, u32[]{:S(2)}, u32[]{:S(2)}) %collective-permute-start.3) | collective-permute-done | bytes 524320 | tf_op jit(solution)/shard_map/ppermute | solution.py:190
  92.1 8.4 %next_camera.3 = (f32[2,1024,128]{2,1,0:T(8,128)S(1)}, f32[2,1024,128]{2,1,0:T(8,128)S(1)}) custom-call(s32[4]{0:T(128)S(1)} %dynamic-slice_reduce_fusion.enabled_ref, bf16[1024,128]{1,0:T(8,128)(2,1)S(1)} %bitcast.14, bf16[2048,128]{1,0:T(8,128)(2,1)S(1)} %collective-permute-done.3.kv_ref, ...), custom_call_target="tpu_custom_call", output_to_operand_aliasing={{0}: (3, {}), {1}: (4, {})} | custom-call | flops 1073741824 | bytes 3145728 | tf_op jit(solution)/shard_map/next_camera/pallas_call | solution.py:164
  100.4 0.0 collective-permute-done.2.kv_ref
  100.4 8.4 %next_camera.4 = (f32[2,1024,128]{2,1,0:T(8,128)S(1)}, f32[2,1024,128]{2,1,0:T(8,128)S(1)}) custom-call(s32[4]{0:T(128)S(1)} %dynamic-slice_reduce_fusion.enabled_ref, bf16[1024,128]{1,0:T(8,128)(2,1)S(1)} %bitcast.15, bf16[2048,128]{1,0:T(8,128)(2,1)S(1)} %collective-permute-done.2.kv_ref, ...), custom_call_target="tpu_custom_call", output_to_operand_aliasing={{0}: (3, {}), {1}: (4, {})} | custom-call | flops 1073741824 | bytes 3145728 | tf_op jit(solution)/shard_map/next_camera/pallas_call | solution.py:164
  108.8 0.0 collective-permute-done.1.kv_ref
  108.8 8.4 %next_camera.5 = (f32[2,1024,128]{2,1,0:T(8,128)S(1)}, f32[2,1024,128]{2,1,0:T(8,128)S(1)}) custom-call(s32[4]{0:T(128)S(1)} %dynamic-slice_reduce_fusion.enabled_ref, bf16[1024,128]{1,0:T(8,128)(2,1)S(1)} %bitcast.16, bf16[2048,128]{1,0:T(8,128)(2,1)S(1)} %collective-permute-done.1.kv_ref, ...), custom_call_target="tpu_custom_call", output_to_operand_aliasing={{0}: (3, {}), {1}: (4, {})} | custom-call | flops 1073741824 | bytes 3145728 | tf_op jit(solution)/shard_map/next_camera/pallas_call | solution.py:164
  117.3 0.0 collective-permute-done.kv_ref
  117.3 8.1 %last_camera.1 = bf16[1024,128]{1,0:T(8,128)(2,1)S(1)} custom-call(s32[4]{0:T(128)S(1)} %dynamic-slice_reduce_fusion.enabled_ref, bf16[1024,128]{1,0:T(8,128)(2,1)S(1)} %bitcast.17, bf16[2048,128]{1,0:T(8,128)(2,1)S(1)} %collective-permute-done.kv_ref, f32[2,1024,128]{2,1,0:T(8,128)S(1)} %get-tuple-element.19.old_sums_ref, ...), custom_call_target="tpu_custom_call" | custom-call | flops 1073741824 | bytes 3145728 | tf_op jit(solution)/shard_map/last_camera/pallas_call | solution.py:177
  125.5 34.6 %all_to_all.15.x_ref = bf16[32,32,128]{2,1,0:T(8,128)(2,1)S(1)} all-to-all(bf16[32,32,128]{2,1,0:T(8,128)(2,1)S(1)} %bitcast.18), channel_id=1, replica_groups=mesh['cam'=16,'seq'=32] {'seq'}, dimensions={0} | all-to-all | bytes 524288 | tf_op jit(solution)/shard_map/all_to_all | solution.py:205
  160.1 0.8 unpack_heads.1
Async XLA Ops:
  0.0 71.5 %copy-start = (s32[16,4]{0,1:T(4,128)S(1)}, s32[16,4]{0,1:T(4,128)}, u32[]{:S(2)}) copy-start(s32[16,4]{0,1:T(4,128)} %param.7) | copy-start | bytes 772
  0.0 1.0 copy-start.2
  1.0 0.9 copy-start.3
  2.9 17.8 %copy-start.1 = (bf16[1,64,2048]{2,1,0:T(8,128)(2,1)S(1)}, bf16[1,64,2048]{2,1,0:T(8,128)(2,1)}, u32[]{:S(2)}) copy-start(bf16[1,64,2048]{2,1,0:T(8,128)(2,1)} %param.4) | copy-start | bytes 786436
  2.9 52.7 %all-to-all-start.1 = ((bf16[32,64,128]{2,1,0:T(8,128)(2,1)}), bf16[32,64,128]{2,1,0:T(8,128)(2,1)S(1)}, u32[]{:S(2)}, u32[]{:S(2)}) async-start(bf16[32,64,128]{2,1,0:T(8,128)(2,1)} %pack_keys_values.1), calls=%async_computation.1 | async-start | bytes 1048576 | tf_op jit(solution)/shard_map/all_to_all | solution.py:196
  55.6 27.5 %all-to-all-start = ((bf16[32,32,128]{2,1,0:T(8,128)(2,1)}), bf16[32,32,128]{2,1,0:T(8,128)(2,1)S(1)}, u32[]{:S(2)}, u32[]{:S(2)}) async-start(bf16[32,32,128]{2,1,0:T(8,128)(2,1)} %pack_queries.1), calls=%async_computation | async-start | bytes 524288 | tf_op jit(solution)/shard_map/all_to_all | solution.py:199
  59.4 32.7 %collective-permute-start.3 = (bf16[2048,128]{1,0:T(8,128)(2,1)S(1)}, bf16[2048,128]{1,0:T(8,128)(2,1)S(1)}, u32[]{:S(2)}, u32[]{:S(2)}) collective-permute-start(bf16[2048,128]{1,0:T(8,128)(2,1)S(1)} %bitcast.7), channel_id=1, source_target_pairs={{0,480},{32,0},{64,32},{96,64},{128,96},{160,128},{192,160},{224,1... | collective-permute-start | bytes 1572872 | tf_op jit(solution)/shard_map/ppermute | solution.py:190
  62.4 38.0 %collective-permute-start.2 = (bf16[2048,128]{1,0:T(8,128)(2,1)S(1)}, bf16[2048,128]{1,0:T(8,128)(2,1)S(1)}, u32[]{:S(2)}, u32[]{:S(2)}) collective-permute-start(bf16[2048,128]{1,0:T(8,128)(2,1)S(1)} %bitcast.8), channel_id=1, source_target_pairs={{0,32},{32,64},{64,96},{96,128},{128,160},{160,192},{192,224},{224... | collective-permute-start | bytes 1572872 | tf_op jit(solution)/shard_map/ppermute | solution.py:190
  64.7 44.2 %collective-permute-start.1 = (bf16[2048,128]{1,0:T(8,128)(2,1)S(1)}, bf16[2048,128]{1,0:T(8,128)(2,1)S(1)}, u32[]{:S(2)}, u32[]{:S(2)}) collective-permute-start(bf16[2048,128]{1,0:T(8,128)(2,1)S(1)} %bitcast.9), channel_id=1, source_target_pairs={{0,448},{32,480},{64,0},{96,32},{128,64},{160,96},{192,128},{224,1... | collective-permute-start | bytes 1572872 | tf_op jit(solution)/shard_map/ppermute | solution.py:190
  68.0 49.3 %collective-permute-start = (bf16[2048,128]{1,0:T(8,128)(2,1)S(1)}, bf16[2048,128]{1,0:T(8,128)(2,1)S(1)}, u32[]{:S(2)}, u32[]{:S(2)}) collective-permute-start(bf16[2048,128]{1,0:T(8,128)(2,1)S(1)} %bitcast.10), channel_id=1, source_target_pairs={{0,64},{32,96},{64,128},{96,160},{128,192},{160,224},{192,256},{22... | collective-permute-start | bytes 1572872 | tf_op jit(solution)/shard_map/ppermute | solution.py:190
where the time goes:
time: 161 us
  waiting for transfers between devices  48.5 us (30%)
  Pallas kernels  42 us (26%)
  blocking collectives  34.6 us (21%)
  starting transfers between devices  33.6 us (21%)
  local copies, waits for them, and re-layouts  2.11 us (1%)
    all_to_all x1, blocking collectives, on_device(): out = lax.all_to_all(out, 'seq', split_axis=0, concat_axis=0, tiled=True)  34.6 us
    all_to_all x1, waiting for transfers between devices, on_device(): lax.all_to_all(kv, 'seq', split_axis=0, concat_axis=0, tiled=True)  34 us
    pallas_call x3, Pallas kernels, next_block(): pl.pallas_call(functools.partial(next_kernel, column), out_shape=(state_s...  25.2 us
    all_to_all x1, starting transfers between devices, on_device(): lax.all_to_all(kv, 'seq', split_axis=0, concat_axis=0, tiled=True)  17.8 us
    ppermute x4, starting transfers between devices, shifted(): lax.ppermute(array, axis, [(i, (i + by) % devices) for i in range(devices)])  12.1 us
    all_to_all x1, waiting for transfers between devices, on_device(): lax.all_to_all(q, 'seq', split_axis=0, concat_axis=0, tiled=True)  11.4 us
    pallas_call x1, Pallas kernels, last_block(): pl.pallas_call(functools.partial(last_kernel, column), out_shape=jax.Shap...  8.14 us
    pallas_call x1, Pallas kernels, first_block(): pl.pallas_call(first_kernel, out_shape=(state_shape(q), state_shape(q)),...  5.94 us
  transfers between devices with their start and end apart: 6, of which 3 were waited for; matrix products, arithmetic and copies ran while one was open for 0% of the time, Pallas kernels for 20%

commit v1 on v0

v1 whole, which is shorter than its diff:
```python
import functools

import jax
import jax.numpy as jnp
from jax import lax
from jax.experimental import pallas as pl
from jax.experimental.pallas import tpu as pltpu
from jax.sharding import PartitionSpec as P

HEADS = 32
HD = 64
WIDE = 2 * HD
TILE = 256
QROWS = 32
LOWEST = -1e30

VMEM = pl.BlockSpec(memory_space=pltpu.VMEM)
SMEM = pl.BlockSpec(memory_space=pltpu.SMEM)


def params(mib):
    return pltpu.CompilerParams(vmem_limit_bytes=mib << 20)


CHUNKS = 4


def side_by_side(out_ref, rows, head, left, right):
    out_ref[head, rows] = jnp.concatenate([left[:, :HD], right[:, :HD]], axis=1)
    out_ref[head + 1, rows] = jnp.concatenate([left[:, HD:], right[:, HD:]], axis=1)


def pack_kernel(q_hbm, k_hbm, v_hbm, out_ref, q_ref, k_ref, v_ref, arrived):
    tokens, width = q_ref.shape
    step = width // CHUNKS
    copies = []
    for chunk in range(CHUNKS):
        columns = pl.ds(chunk * step, step)
        for place, (far, near) in enumerate(((k_hbm, k_ref), (v_hbm, v_ref), (q_hbm, q_ref))):
            copy = pltpu.make_async_copy(far.at[:, columns], near.at[:, columns], arrived.at[chunk, place])
            copy.start()
            copies.append(copy)
    half = tokens // 2
    for chunk in range(CHUNKS):
        for copy in copies[3 * chunk : 3 * chunk + 3]:
            copy.wait()
        for start in range(chunk * step, (chunk + 1) * step, WIDE):
            columns = pl.ds(start, WIDE)
            head = start // HD
            side_by_side(out_ref, pl.ds(0, tokens), head, k_ref[:, columns], v_ref[:, columns])
            upper, lower = q_ref[pl.ds(0, half), columns], q_ref[pl.ds(half, half), columns]
            side_by_side(out_ref, pl.ds(tokens, half), head, upper, lower)


def pack_heads(queries, keys, values):
    tokens, width = keys.shape
    held = pltpu.VMEM((tokens, width), keys.dtype)
    return pl.pallas_call(
        pack_kernel,
        out_shape=jax.ShapeDtypeStruct((HEADS, tokens + tokens // 2, WIDE), keys.dtype),
        in_specs=[pl.BlockSpec(memory_space=pl.ANY)] * 3,
        out_specs=VMEM,
        scratch_shapes=[held, held, held, pltpu.SemaphoreType.DMA((CHUNKS, 3))],
        compiler_params=params(60),
        name="pack_heads",
    )(queries, keys, values)


def unpack_kernel(x_ref, out_ref):
    half = x_ref.shape[1]
    for pair in range(HEADS // 2):
        even, odd = x_ref[2 * pair], x_ref[2 * pair + 1]
        columns = pl.ds(pair * WIDE, WIDE)
        out_ref[pl.ds(0, half), columns] = jnp.concatenate([even[:, :HD], odd[:, :HD]], axis=1)
        out_ref[pl.ds(half, half), columns] = jnp.concatenate([even[:, HD:], odd[:, HD:]], axis=1)


def unpack_heads(x):
    return pl.pallas_call(
        unpack_kernel,
        out_shape=jax.ShapeDtypeStruct((2 * x.shape[1], HEADS * HD), x.dtype),
        in_specs=[VMEM],
        out_specs=VMEM,
        compiler_params=params(16),
        name="unpack_heads",
    )(x)


def tile_scores(packed_ref, rows, half, keys):
    sources = TILE // QROWS
    queries = packed_ref[rows // QROWS : rows // QROWS + sources, 2 * QROWS :, half * HD : (half + 1) * HD]
    queries = queries.reshape(TILE, HD) * jnp.bfloat16(HD**-0.5)
    return lax.dot_general(queries, keys, (((1,), (1,)), ((), ())), preferred_element_type=jnp.float32)


def keys_and_values(kv):
    lane = lax.broadcasted_iota(jnp.int32, kv.shape, 1)
    return kv[:, :HD], jnp.where(lane < HD, jnp.bfloat16(1), kv)


def attend(packed_ref, kv_ref, old_peaks, store):
    keys, values = keys_and_values(kv_ref[...])
    units = [(rows, half) for rows in range(0, packed_ref.shape[0] * QROWS, TILE) for half in range(2)]

    def blend(rows, half, peak, old_peak, weights):
        store(rows, half, peak, old_peak, jnp.dot(weights, values, preferred_element_type=jnp.float32))

    scores = tile_scores(packed_ref, *units[0], keys)
    waiting = None
    for place, (rows, half) in enumerate(units):
        ahead = tile_scores(packed_ref, *units[place + 1], keys) if place + 1 < len(units) else None
        peak = jnp.max(scores, axis=1, keepdims=True)
        old_peak = None
        if old_peaks is not None:
            old_peak = old_peaks[half, pl.ds(rows, TILE)]
            peak = jnp.maximum(peak, old_peak)
        weights = jnp.exp(scores - peak[:, :1]).astype(jnp.bfloat16)
        if waiting is not None:
            blend(*waiting)
        waiting = (rows, half, peak, old_peak, weights)
        scores = ahead
    blend(*waiting)


def update(packed_ref, kv_ref, old_sums, old_peaks, sums, peaks):
    def store(rows, half, peak, old_peak, added):
        rows = pl.ds(rows, TILE)
        if old_peak is not None:
            added = old_sums[half, rows] * jnp.exp(old_peak - peak) + added
        sums[half, rows] = added
        peaks[half, rows] = jnp.broadcast_to(peak, (TILE, WIDE))

    attend(packed_ref, kv_ref, old_peaks, store)


def own_kernel(packed_ref, kv_ref, sums, peaks, mark):
    update(packed_ref, kv_ref, None, None, sums, peaks)
    mark[...] = jnp.zeros_like(mark)


def near_kernel(columns, mask_ref, packed_ref, one_ref, two_ref, _, sums, peaks):
    @pl.when(mask_ref[columns[0]] > 0)
    def _():
        update(packed_ref, one_ref, None, None, sums, peaks)

    @pl.when(mask_ref[columns[0]] <= 0)
    def _():
        sums[...] = jnp.zeros_like(sums)
        peaks[...] = jnp.full_like(peaks, LOWEST)

    @pl.when(mask_ref[columns[1]] > 0)
    def _():
        update(packed_ref, two_ref, sums, peaks, sums, peaks)


def far_kernel(
    columns, mask_ref, packed_ref, one_ref, two_ref, own_sums, own_peaks, near_sums, near_peaks, out_ref, sums, peaks
):
    @pl.when(mask_ref[columns[0]] > 0)
    def _():
        update(packed_ref, one_ref, near_sums, near_peaks, sums, peaks)

    @pl.when(mask_ref[columns[0]] <= 0)
    def _():
        sums[...] = near_sums[...]
        peaks[...] = near_peaks[...]

    def finish(rows, half, parts):
        parts = parts + [(own_sums[half, rows], own_peaks[half, rows]), (sums[half, rows], peaks[half, rows])]
        highest = functools.reduce(jnp.maximum, [part[1] for part in parts])
        total = sum(part[0] * jnp.exp(part[1] - highest) for part in parts)
        out_ref[rows, half * HD : (half + 1) * HD] = (total[:, HD:] / total[:, :HD]).astype(out_ref.dtype)

    def store(rows, half, peak, old_peak, added):
        finish(pl.ds(rows, TILE), half, [(added, jnp.broadcast_to(peak, added.shape))])

    @pl.when(mask_ref[columns[1]] > 0)
    def _():
        attend(packed_ref, two_ref, None, store)

    @pl.when(mask_ref[columns[1]] <= 0)
    def _():
        for start in range(0, out_ref.shape[0], TILE):
            for half in range(2):
                finish(pl.ds(start, TILE), half, [])


def cost(packed, blocks):
    pairs = blocks * (packed.shape[0] * 2 * QROWS) ** 2
    return pl.CostEstimate(flops=4 * pairs * HD, bytes_accessed=3 << 20, transcendentals=pairs)


def state_shape(packed):
    return jax.ShapeDtypeStruct((2, packed.shape[0] * QROWS, WIDE), jnp.float32)


def own_camera(packed, kv):
    return pl.pallas_call(
        own_kernel,
        out_shape=(state_shape(packed), state_shape(packed), jax.ShapeDtypeStruct((8, WIDE), jnp.float32)),
        in_specs=[VMEM, VMEM],
        out_specs=(VMEM, VMEM, VMEM),
        compiler_params=params(32),
        cost_estimate=cost(packed, 1),
        name="own_camera",
    )(packed, kv)


def near_cameras(columns, mask, packed, one, two, mark):
    return pl.pallas_call(
        functools.partial(near_kernel, columns),
        out_shape=(state_shape(packed), state_shape(packed)),
        in_specs=[SMEM] + [VMEM] * 4,
        out_specs=(VMEM, VMEM),
        compiler_params=params(32),
        cost_estimate=cost(packed, 2),
        name="near_cameras",
    )(mask, packed, one, two, mark)


def far_cameras(columns, mask, packed, one, two, own, near):
    state = pltpu.VMEM(near[0].shape, near[0].dtype)
    return pl.pallas_call(
        functools.partial(far_kernel, columns),
        out_shape=jax.ShapeDtypeStruct((near[0].shape[1], WIDE), packed.dtype),
        in_specs=[SMEM] + [VMEM] * 7,
        out_specs=VMEM,
        scratch_shapes=[state, state],
        compiler_params=params(32),
        cost_estimate=cost(packed, 2),
        name="far_cameras",
    )(mask, packed, one, two, *own, *near)


def swapped(array, axis, first):
    devices = lax.axis_size(axis)
    pairs = [(i % devices, (i + 1) % devices) for i in range(first, first + devices, 2)]
    return lax.ppermute(array, axis, pairs + [(j, i) for i, j in pairs])


def on_device(queries, keys, values, neighbour_mask):
    camera = lax.axis_index("cam")
    own_row = lax.dynamic_index_in_dim(neighbour_mask, camera, 0, keepdims=False)
    own_row = jnp.where(camera % 2 == 0, own_row, jnp.roll(own_row, 2))
    packed = pack_heads(queries[0], keys[0], values[0])
    packed = lax.all_to_all(packed, "seq", split_axis=0, concat_axis=0, tiled=True)
    kv = packed[:, : 2 * QROWS].reshape(-1, WIDE)
    one, two = swapped(kv, "cam", 0), swapped(kv, "cam", 1)
    *own, mark = own_camera(packed, kv)
    one, mark = lax.optimization_barrier((one, mark))
    far_two, far_one = swapped(one, "cam", 1), swapped(two, "cam", 0)
    near = near_cameras((0, 2), own_row, packed, one, two, mark)
    out = far_cameras((3, 1), own_row, packed, far_two, far_one, own, near)
    out = out.reshape(HEADS, QROWS, WIDE)
    out = lax.all_to_all(out, "seq", split_axis=0, concat_axis=0, tiled=True)
    return unpack_heads(out)[None]


def solution(mesh):
    return jax.shard_map(
        on_device,
        mesh=mesh,
        in_specs=(P("cam", "seq", None), P("cam", "seq", None), P("cam", "seq", None), P()),
        out_specs=P("cam", "seq", None),
        check_vma=False,
    )
```

time: 161 us -> 139 us (0.86)
  the two profiles are of different devices: /device:TPU:33 before, /device:TPU:1 now
where the time goes in v1:
time: 139 us; the launch traced here: 138 us
  blocking collectives  85.5 us (62%)
  Pallas kernels  25.3 us (18%)
  starting transfers between devices  18.9 us (14%)
  waiting for transfers between devices  7.21 us (5%)
    all_to_all x1, blocking collectives, on_device(): lax.all_to_all(packed, 'seq', split_axis=0, concat_axis=0, tiled=True)  58.3 us
    all_to_all x1, blocking collectives, on_device(): out = lax.all_to_all(out, 'seq', split_axis=0, concat_axis=0, tiled=True)  27.2 us
    ppermute x4, starting transfers between devices, swapped(): return lax.ppermute(array, axis, pairs + [(j, i) for i, j in pairs])  18.9 us
    pallas_call x1, Pallas kernels, far_cameras(): pl.pallas_call(functools.partial(far_kernel, columns), out_shape=jax.Shap...  11.4 us
    ppermute x4, waiting for transfers between devices, swapped(): return lax.ppermute(array, axis, pairs + [(j, i) for i, j in pairs])  7.21 us
    pallas_call x1, Pallas kernels, near_cameras(): pl.pallas_call(functools.partial(near_kernel, columns), out_shape=(state_...  5.8 us
    pallas_call x1, Pallas kernels, own_camera(): pl.pallas_call(own_kernel, out_shape=(state_shape(packed), state_shape(pa...  4.9 us
  transfers between devices with their start and end apart: 4, of which 3 were waited for; matrix products, arithmetic and copies ran while one was open for 0% of the time, Pallas kernels for 8%

profile of v1, /device:TPU:1, one launch (start us, length us, event | category | flops | bytes accessed | tf_op | source)
XLA Modules:
  0.0 138.2 jit_solution(1691366854816093238)
XLA Ops:
  0.0 2.4 %pack_heads.1 = bf16[32,96,128]{2,1,0:T(8,128)(2,1)} custom-call(bf16[64,2048]{1,0:T(8,128)(2,1)} %bitcast.10, bf16[64,2048]{1,0:T(8,128)(2,1)} %bitcast.11, bf16[64,2048]{1,0:T(8,128)(2,1)} %bitcast.12), custom_call_target="tpu_custom_call" | custom-call | tf_op jit(solution)/shard_map/pack_heads/pallas_call | solution.py:58
  2.4 58.3 %all_to_all.10.packed_ref = bf16[32,96,128]{2,1,0:T(8,128)(2,1)S(1)} all-to-all(bf16[32,96,128]{2,1,0:T(8,128)(2,1)} %pack_heads.1), channel_id=1, replica_groups=mesh['cam'=16,'seq'=32] {'seq'}, dimensions={0} | all-to-all | bytes 1572864 | tf_op jit(solution)/shard_map/all_to_all | solution.py:246
  60.7 0.1 slice.22
  60.7 3.1 %collective-permute-start = (bf16[2048,128]{1,0:T(8,128)(2,1)S(1)}, bf16[2048,128]{1,0:T(8,128)(2,1)S(1)}, u32[]{:S(2)}, u32[]{:S(2)}) collective-permute-start(bf16[2048,128]{1,0:T(8,128)(2,1)S(1)} %bitcast.6), channel_id=1, source_target_pairs={{0,32},{64,96},{128,160},{192,224},{256,288},{320,352},{384,416},{... | collective-permute-start | bytes 1572872 | tf_op jit(solution)/shard_map/ppermute | solution.py:238
  63.9 10.7 %collective-permute-start.2 = (bf16[2048,128]{1,0:T(8,128)(2,1)S(1)}, bf16[2048,128]{1,0:T(8,128)(2,1)S(1)}, u32[]{:S(2)}, u32[]{:S(2)}) collective-permute-start(bf16[2048,128]{1,0:T(8,128)(2,1)S(1)} %bitcast.7), channel_id=1, source_target_pairs={{32,64},{96,128},{160,192},{224,256},{288,320},{352,384},{416,448}... | collective-permute-start | bytes 1572872 | tf_op jit(solution)/shard_map/ppermute | solution.py:238
  74.6 0.0 copy-start
  74.6 0.7 copy-done
  75.3 0.2 fusion
  75.5 4.9 %own_camera.1 = (f32[2,1024,128]{2,1,0:T(8,128)S(1)}, f32[2,1024,128]{2,1,0:T(8,128)S(1)}, f32[8,128]{1,0:T(8,128)S(1)}) custom-call(bf16[32,96,128]{2,1,0:T(8,128)(2,1)S(1)} %all_to_all.10.packed_ref, bf16[2048,128]{1,0:T(8,128)(2,1)S(1)} %bitcast.8), custom_call_target="tpu_custom_call" | custom-call | flops 1073741824 | bytes 3145728 | tf_op jit(solution)/shard_map/own_camera/pallas_call | solution.py:198
  80.4 0.0 collective-permute-done.one_ref
  80.4 3.2 %collective-permute-start.1 = (bf16[2048,128]{1,0:T(8,128)(2,1)S(1)}, bf16[2048,128]{1,0:T(8,128)(2,1)S(1)}, u32[]{:S(2)}, u32[]{:S(2)}) collective-permute-start(bf16[2048,128]{1,0:T(8,128)(2,1)S(1)} %collective-permute-done.one_ref), channel_id=1, source_target_pairs={{32,64},{96,128},{160,192},{224,256},{288,320},{352,384},{416,448}... | collective-permute-start | bytes 1572872 | tf_op jit(solution)/shard_map/ppermute | solution.py:238
  83.6 0.9 collective-permute-done.2.two_ref
  84.5 1.9 %collective-permute-start.3 = (bf16[2048,128]{1,0:T(8,128)(2,1)S(1)}, bf16[2048,128]{1,0:T(8,128)(2,1)S(1)}, u32[]{:S(2)}, u32[]{:S(2)}) collective-permute-start(bf16[2048,128]{1,0:T(8,128)(2,1)S(1)} %collective-permute-done.2.two_ref), channel_id=1, source_target_pairs={{0,32},{64,96},{128,160},{192,224},{256,288},{320,352},{384,416},{... | collective-permute-start | bytes 1572872 | tf_op jit(solution)/shard_map/ppermute | solution.py:238
  86.4 0.1 slice_reduce_fusion.1
  86.5 0.1 broadcast_select_fusion.mask_ref
  86.6 5.8 %near_cameras.1 = (f32[2,1024,128]{2,1,0:T(8,128)S(1)}, f32[2,1024,128]{2,1,0:T(8,128)S(1)}) custom-call(s32[4]{0:T(128)S(1)} %broadcast_select_fusion.mask_ref, bf16[32,96,128]{2,1,0:T(8,128)(2,1)S(1)} %all_to_all.10.packed_ref, bf16[2048,128]{1,0:T(8,128)(2,1)S(1)} %collective-permute-done.one_ref, bf16[2048,128]{1,0:T(8,128)(2,1)S(1)} %collective-permute-done.2.two_ref, ...), custom_call_target="tpu_custom_call" | custom-call | flops 2147483648 | bytes 3145728 | tf_op jit(solution)/shard_map/near_cameras/pallas_call | solution.py:210
  92.4 4.5 %collective-permute-done.1.one_ref = bf16[2048,128]{1,0:T(8,128)(2,1)S(1)} collective-permute-done((bf16[2048,128]{1,0:T(8,128)(2,1)S(1)}, bf16[2048,128]{1,0:T(8,128)(2,1)S(1)}, u32[]{:S(2)}, u32[]{:S(2)}) %collective-permute-start.1) | collective-permute-done | bytes 524320 | tf_op jit(solution)/shard_map/ppermute | solution.py:238
  96.9 1.9 %collective-permute-done.3.two_ref = bf16[2048,128]{1,0:T(8,128)(2,1)S(1)} collective-permute-done((bf16[2048,128]{1,0:T(8,128)(2,1)S(1)}, bf16[2048,128]{1,0:T(8,128)(2,1)S(1)}, u32[]{:S(2)}, u32[]{:S(2)}) %collective-permute-start.3) | collective-permute-done | bytes 524320 | tf_op jit(solution)/shard_map/ppermute | solution.py:238
  98.8 11.4 %far_cameras.1 = bf16[1024,128]{1,0:T(8,128)(2,1)S(1)} custom-call(s32[4]{0:T(128)S(1)} %broadcast_select_fusion.mask_ref, bf16[32,96,128]{2,1,0:T(8,128)(2,1)S(1)} %all_to_all.10.packed_ref, bf16[2048,128]{1,0:T(8,128)(2,1)S(1)} %collective-permute-done.1.one_ref, bf16[2048,128]{1,0:T(8,128)(2,1)S(1)} %collective-permute-done.3.two_ref, ...), custom_call_target="tpu_custom_call" | custom-call | flops 2147483648 | bytes 3145728 | tf_op jit(solution)/shard_map/far_cameras/pallas_call | solution.py:223
  110.1 27.2 %all_to_all.11.x_ref = bf16[32,32,128]{2,1,0:T(8,128)(2,1)S(1)} all-to-all(bf16[32,32,128]{2,1,0:T(8,128)(2,1)S(1)} %bitcast.9), channel_id=1, replica_groups=mesh['cam'=16,'seq'=32] {'seq'}, dimensions={0} | all-to-all | bytes 524288 | tf_op jit(solution)/shard_map/all_to_all | solution.py:255
  137.4 0.8 unpack_heads.1
Async XLA Ops:
  60.7 19.6 %collective-permute-start = (bf16[2048,128]{1,0:T(8,128)(2,1)S(1)}, bf16[2048,128]{1,0:T(8,128)(2,1)S(1)}, u32[]{:S(2)}, u32[]{:S(2)}) collective-permute-start(bf16[2048,128]{1,0:T(8,128)(2,1)S(1)} %bitcast.6), channel_id=1, source_target_pairs={{0,32},{64,96},{128,160},{192,224},{256,288},{320,352},{384,416},{... | collective-permute-start | bytes 1572872 | tf_op jit(solution)/shard_map/ppermute | solution.py:238
  63.9 20.6 %collective-permute-start.2 = (bf16[2048,128]{1,0:T(8,128)(2,1)S(1)}, bf16[2048,128]{1,0:T(8,128)(2,1)S(1)}, u32[]{:S(2)}, u32[]{:S(2)}) collective-permute-start(bf16[2048,128]{1,0:T(8,128)(2,1)S(1)} %bitcast.7), channel_id=1, source_target_pairs={{32,64},{96,128},{160,192},{224,256},{288,320},{352,384},{416,448}... | collective-permute-start | bytes 1572872 | tf_op jit(solution)/shard_map/ppermute | solution.py:238
  74.6 0.7 copy-start
  80.4 16.5 %collective-permute-start.1 = (bf16[2048,128]{1,0:T(8,128)(2,1)S(1)}, bf16[2048,128]{1,0:T(8,128)(2,1)S(1)}, u32[]{:S(2)}, u32[]{:S(2)}) collective-permute-start(bf16[2048,128]{1,0:T(8,128)(2,1)S(1)} %collective-permute-done.one_ref), channel_id=1, source_target_pairs={{32,64},{96,128},{160,192},{224,256},{288,320},{352,384},{416,448}... | collective-permute-start | bytes 1572872 | tf_op jit(solution)/shard_map/ppermute | solution.py:238
  84.5 14.3 %collective-permute-start.3 = (bf16[2048,128]{1,0:T(8,128)(2,1)S(1)}, bf16[2048,128]{1,0:T(8,128)(2,1)S(1)}, u32[]{:S(2)}, u32[]{:S(2)}) collective-permute-start(bf16[2048,128]{1,0:T(8,128)(2,1)S(1)} %collective-permute-done.2.two_ref), channel_id=1, source_target_pairs={{0,32},{64,96},{128,160},{192,224},{256,288},{320,352},{384,416},{... | collective-permute-start | bytes 1572872 | tf_op jit(solution)/shard_map/ppermute | solution.py:238
